TPU v7x, 512 devices: a whole 4x4x16 slice. The times are simulated.
512 devices in a mesh: slab: 16 (over z_lo, y), rcv: 32 (over x, z_hi, core).
Axes of the slice: x: 4, y: 4, z: 16 (z_hi: 4, z_lo: 4; z = z_hi * 4 + z_lo), core: 2. Of those that a mesh axis runs over, the one named last changes fastest.
Arguments:
- adjoint_now: float32 [32, 64, 128, 128], P('rcv', 'slab'), may hold values from -6 to 6
- adjoint_before: float32 [32, 64, 128, 128], P('rcv', 'slab'), may hold values from -6 to 6
- courant_field: float32 [64, 128, 128], P('slab'), may hold values from 0.04 to 0.2
- log_buoyancy: float32 [64, 128, 128], P('slab'), may hold values from -0.3 to 0.3
- snapshot_store: float32 [32, 64, 128, 128], P('rcv', 'slab'), may hold values from -6 to 6
- owner_order: int32 [32], replicated, may hold values from 0 to 31, each once
- receiver_cells: int32 [32], P('rcv'), may hold values from 0 to 1048575
- receiver_traces: float32 [32, 8], P('rcv'), may hold values from -6 to 6
- residual_weights: float32 [32], P('rcv'), may hold values from -0.3 to 0.3
Outputs:
- sensitivity: float32 [64, 128, 128], P('slab', 'rcv')
- adjoint_after: float32 [32, 64, 128, 128], P('rcv', 'slab')
Inputs may be any that keep to these rules, and one draw needn't show every extreme that they name: Each slot number appears once; checkpoint k reads slot owner_order[k] for k < 4. `receiver_cells`: a cell of the grid.
All inputs are finite; a program needn't handle non-finite values.
Results may differ from a plain program's by a relative error of at most 0.0003.
Values sent between devices are 32-bit elements; how exact they have to be, the bound alone decides.
A program may use at most 64 MiB of HBM per device.

v0:
```python
import jax
import jax.numpy as jnp
from jax import lax
from jax.sharding import PartitionSpec as P

SNAPS = 4


def extended(shard, sides, width):
    for axis, dim in sides:
        peers, length = (lax.axis_size(axis), shard.shape[dim])
        up = [(i, (i + 1) % peers) for i in range(peers - 1)]
        down = [(j, i) for i, j in up]
        last = lax.slice_in_dim(shard, length - width, length, axis=dim)
        leading = lax.slice_in_dim(shard, 0, width, axis=dim)
        before = lax.ppermute(last, axis, up)
        after = lax.ppermute(leading, axis, down)
        shard = jnp.concatenate([before, shard, after], axis=dim)
    return shard


def from_root(block, axis, owner):
    block = jnp.where(lax.axis_index(axis) == owner, block, jnp.zeros_like(block))
    return lax.psum(block, axis)


def piece_of(field, axis_no, begin, extent):
    return lax.slice_in_dim(field, begin, begin + extent, axis=axis_no)


def pad_axis(field, axis_no):
    widths = [(0, 0)] * field.ndim
    widths[axis_no] = (2, 2)
    return jnp.pad(field, widths)


def second_diff(field, axis_no, extent):
    outer = piece_of(field, axis_no, 0, extent) + piece_of(field, axis_no, 4, extent)
    inner = piece_of(field, axis_no, 1, extent) + piece_of(field, axis_no, 3, extent)
    return (16.0 * inner - outer - 30.0 * piece_of(field, axis_no, 2, extent)) / 12.0


def first_diff(field, axis_no, extent):
    inner = piece_of(field, axis_no, 3, extent) - piece_of(field, axis_no, 1, extent)
    outer = piece_of(field, axis_no, 4, extent) - piece_of(field, axis_no, 0, extent)
    return (8.0 * inner - outer) / 12.0


def slopes(log_ext):
    width = log_ext.shape[0] - 4
    centre = piece_of(log_ext, 0, 2, width)
    wide_y = pad_axis(centre, 1)
    wide_z = pad_axis(centre, 2)
    return jnp.stack(
        [
            first_diff(log_ext, 0, width),
            first_diff(wide_y, 1, centre.shape[1]),
            first_diff(wide_z, 2, centre.shape[2]),
        ]
    )


def advance(field, before, courant, gradient):
    first_axis = field.ndim - 3
    width = field.shape[first_axis] - 4
    centre = piece_of(field, first_axis, 2, width)
    wide_y = pad_axis(centre, first_axis + 1)
    wide_z = pad_axis(centre, first_axis + 2)
    size_y = field.shape[first_axis + 1]
    size_z = field.shape[first_axis + 2]
    curvature = (
        second_diff(field, first_axis, width)
        + second_diff(wide_y, first_axis + 1, size_y)
        + second_diff(wide_z, first_axis + 2, size_z)
    )
    drift_term = (
        gradient[0] * first_diff(field, first_axis, width)
        + gradient[1] * first_diff(wide_y, first_axis + 1, size_y)
        + gradient[2] * first_diff(wide_z, first_axis + 2, size_z)
    )
    return 2.0 * centre - before + courant * (curvature + drift_term)


def local(
    adjoint_now,
    adjoint_before,
    courant_field,
    log_buoyancy,
    snapshot_store,
    owner_order,
    receiver_cells,
    receiver_traces,
    residual_weights,
):
    slab_rows = courant_field.shape[0]
    size_y = courant_field.shape[1]
    size_z = courant_field.shape[2]
    grid_rows = slab_rows * lax.axis_size("slab")
    row_anchor = lax.axis_index("slab") * slab_rows
    model_ext = extended(jnp.stack([courant_field, log_buoyancy]), (("slab", 1),), 4)
    courant_ext = model_ext[0, 2 : slab_rows + 6]
    gradient = slopes(model_ext[1])
    plane_ids = lax.broadcasted_iota(
        jnp.int32, (size_y, size_z), 0
    ) * size_z + lax.broadcasted_iota(jnp.int32, (size_y, size_z), 1)
    cell_column = receiver_cells[:, None, None, None]

    def evolve(field, before, offset, width, tick):
        upcoming = advance(
            field,
            before,
            courant_ext[offset - 2 : offset - 2 + width],
            gradient[:, offset - 2 : offset - 2 + width],
        )
        global_rows = row_anchor - 4 + offset + lax.broadcasted_iota(jnp.int32, (width,), 0)
        flat_ids = global_rows[:, None, None] * (size_y * size_z) + plane_ids[None]
        amplitude = receiver_traces[:, tick][:, None, None, None]
        upcoming = upcoming + jnp.where(flat_ids[None] == cell_column, amplitude, 0.0)
        return (upcoming, global_rows)

    current = adjoint_now
    previous = adjoint_before
    kernel_sum = jnp.zeros((slab_rows, size_y, size_z), jnp.float32)
    for snap_index in range(SNAPS):
        forward_field = from_root(snapshot_store[0], "rcv", owner_order[snap_index])
        current_ext = extended(current, (("slab", 1),), 4)
        previous_ext = extended(previous, (("slab", 1),), 2)
        middle, middle_rows = evolve(current_ext, previous_ext, 2, slab_rows + 4, 2 * snap_index)
        inside = (middle_rows >= 0) & (middle_rows < grid_rows)
        middle = jnp.where(inside[None, :, None, None], middle, 0.0)
        latest, unused_rows = evolve(middle, current, 4, slab_rows, 2 * snap_index + 1)
        previous = middle[:, 2 : slab_rows + 2]
        current = latest
        kernel_terms = jnp.sum(
            residual_weights[:, None, None, None] * current * forward_field, axis=0
        )
        kernel_sum = kernel_sum + kernel_terms
    sensitivity = lax.psum_scatter(kernel_sum, "rcv", scatter_dimension=1, tiled=True)
    return (sensitivity, current)


def solution(mesh):
    placed = (
        P("rcv", "slab", None, None),
        P("rcv", "slab", None, None),
        P("slab", None, None),
        P("slab", None, None),
        P("rcv", "slab", None, None),
        P(),
        P("rcv"),
        P("rcv", None),
        P("rcv"),
    )
    return jax.shard_map(
        local,
        mesh=mesh,
        in_specs=placed,
        out_specs=(P("slab", "rcv", None), P("rcv", "slab", None, None)),
        check_vma=False,
    )
```

profile of v0, /device:TPU:1, one launch (start us, length us, event | category | flops | bytes accessed | tf_op | source)
XLA Modules:
  0.0 783.1 jit_solution(6446867127906794386)
XLA Ops:
  8.3 4.1 collective-permute-start.4
  13.7 4.0 collective-permute-start
  20.7 4.6 collective-permute-start.2
  30.3 4.7 collective-permute-done.3
  34.9 3.5 fusion.12
  38.5 2.0 fusion.37
  40.5 4.1 collective-permute-start.6
  50.2 4.0 collective-permute-start.8
  56.7 5.1 collective-permute-done.9
  61.8 2.9 fusion.15
  64.8 2.9 fusion.34
  67.6 4.3 collective-permute-start.10
  75.4 4.1 collective-permute-start.12
  82.0 5.3 collective-permute-done.13
  87.3 3.0 fusion.18
  90.4 2.2 fusion.31
  92.5 4.2 collective-permute-start.14
  98.7 4.6 collective-permute-start.16
  104.7 1.8 collective-permute-done.16
  106.5 5.7 collective-permute-done.17
  112.2 1.8 fusion.21
  114.8 318.7 %all-reduce.25.cloned.1.call-done = (f32[1,4,128,128]{3,2,1,0:T(8,128)}, f32[1,4,128,128]{3,2,1,0:T(8,128)}, f32[1,4,128,128]{3,2,1,0:T(8,128)}, f32[1,4,128,128]{3,2,1,0:T(8,128)}) async-done(((f32[1,4,128,128]{3,2,1,0:T(8,128)}, f32[1,4,128,128]{3,2,1,0:T(8,128)}, f32[1,4,128,128]{3,2,1,0:T(8,128)}, f32[1,4,128,128]{3,2,1,0:T(8,128)}), (f32[1,4,128,128]{3,2,1,0:T(8,128)}, f32[1,4,128,128]{3,2,1,0:T(8,128)}, ...) | async-done | bytes 1048592 | tf_op jit(solution)/shard_map/psum | solution.py:24
  433.5 3.8 add_bitcast_fusion
  439.2 335.7 %all-reduce.23.cloned.1.call-done = f32[4,128,128]{2,1,0:T(8,128)} async-done(((f32[4,128,128]{2,1,0:T(8,128)}), f32[4,128,128]{2,1,0:T(8,128)}) %all-reduce.23.cloned.1.call-update) | async-done | bytes 262160
  (93 shorter events, 27.1 us)
Async XLA Ops:
  7.2 21.0 %copy-start.13 = (f32[1,4,128,128]{3,2,1,0:T(8,128)S(1)}, f32[1,4,128,128]{3,2,1,0:T(8,128)}, u32[]{:S(2)}) copy-start(f32[1,4,128,128]{3,2,1,0:T(8,128)} %param.9) | copy-start | bytes 786436
  7.2 18.2 %copy-start.16 = (f32[1,8]{1,0:T(1,128)S(1)}, f32[1,8]{1,0:T(1,128)}, u32[]{:S(2)}) copy-start(f32[1,8]{1,0:T(1,128)} %param.16) | copy-start | bytes 100
  7.2 426.3 %all-reduce.25.cloned.1.call-start = ((), (), s32[]{:S(2)}) async-start(), calls=%async_computation.1 | async-start | bytes 2097152 | tf_op jit(solution)/shard_map/psum | solution.py:24
  8.3 21.0 %collective-permute-start.4 = (f32[2,4,128,128]{3,2,1,0:T(8,128)S(1)}, f32[2,4,128,128]{3,2,1,0:T(8,128)S(1)}, u32[]{:S(2)}, u32[]{:S(2)}) collective-permute-start(f32[2,4,128,128]{3,2,1,0:T(8,128)S(1)} %pad_maximum_fusion.8), channel_id=1, source_target_pairs={{0,32},{32,64},{64,96},{96,128},{128,160},{160,192},{192,224},{224... | collective-permute-start | bytes 1572872 | tf_op jit(solution)/shard_map/ppermute | solution.py:16
  12.4 16.9 %collective-permute-start.5 = (f32[2,4,128,128]{3,2,1,0:T(8,128)S(1)}, f32[2,4,128,128]{3,2,1,0:T(8,128)S(1)}, u32[]{:S(2)}, u32[]{:S(2)}) collective-permute-start(f32[2,4,128,128]{3,2,1,0:T(8,128)S(1)} %pad_maximum_fusion.8), channel_id=1, source_target_pairs={{32,0},{64,32},{96,64},{128,96},{160,128},{192,160},{224,192},{256... | collective-permute-start | bytes 1572872 | tf_op jit(solution)/shard_map/ppermute | solution.py:17
  13.7 13.1 %collective-permute-start = (f32[1,4,128,128]{3,2,1,0:T(8,128)}, f32[1,4,128,128]{3,2,1,0:T(8,128)S(1)}, u32[]{:S(2)}, u32[]{:S(2)}) collective-permute-start(f32[1,4,128,128]{3,2,1,0:T(8,128)} %param.9), channel_id=1, source_target_pairs={{0,32},{32,64},{64,96},{96,128},{128,160},{160,192},{192,224},{224... | collective-permute-start | bytes 786440 | tf_op jit(solution)/shard_map/ppermute | solution.py:16
  17.7 11.5 %collective-permute-start.1 = (f32[1,4,128,128]{3,2,1,0:T(8,128)}, f32[1,4,128,128]{3,2,1,0:T(8,128)S(1)}, u32[]{:S(2)}, u32[]{:S(2)}) collective-permute-start(f32[1,4,128,128]{3,2,1,0:T(8,128)} %param.9), channel_id=1, source_target_pairs={{32,0},{64,32},{96,64},{128,96},{160,128},{192,160},{224,192},{256... | collective-permute-start | bytes 786440 | tf_op jit(solution)/shard_map/ppermute | solution.py:17
  20.7 9.6 %collective-permute-start.2 = (f32[1,2,128,128]{3,2,1,0:T(8,128)}, f32[1,2,128,128]{3,2,1,0:T(8,128)}, u32[]{:S(2)}, u32[]{:S(2)}) collective-permute-start(f32[1,2,128,128]{3,2,1,0:T(8,128)} %get-tuple-element.25), channel_id=1, source_target_pairs={{0,32},{32,64},{64,96},{96,128},{128,160},{160,192},{192,224},{224... | collective-permute-start | bytes 393224 | tf_op jit(solution)/shard_map/ppermute | solution.py:16
  26.8 8.2 %collective-permute-start.3 = (f32[1,2,128,128]{3,2,1,0:T(8,128)}, f32[1,2,128,128]{3,2,1,0:T(8,128)S(1)}, u32[]{:S(2)}, u32[]{:S(2)}) collective-permute-start(f32[1,2,128,128]{3,2,1,0:T(8,128)} %get-tuple-element.26), channel_id=1, source_target_pairs={{32,0},{64,32},{96,64},{128,96},{160,128},{192,160},{224,192},{256... | collective-permute-start | bytes 393224 | tf_op jit(solution)/shard_map/ppermute | solution.py:17
  40.5 15.0 %collective-permute-start.6 = (f32[1,4,128,128]{3,2,1,0:T(8,128)}, f32[1,4,128,128]{3,2,1,0:T(8,128)}, u32[]{:S(2)}, u32[]{:S(2)}) collective-permute-start(f32[1,4,128,128]{3,2,1,0:T(8,128)} %fusion.37), channel_id=1, source_target_pairs={{0,32},{32,64},{64,96},{96,128},{128,160},{160,192},{192,224},{224... | collective-permute-start | bytes 786440 | tf_op jit(solution)/shard_map/ppermute | solution.py:16
  44.6 10.9 %collective-permute-start.7 = (f32[1,4,128,128]{3,2,1,0:T(8,128)}, f32[1,4,128,128]{3,2,1,0:T(8,128)}, u32[]{:S(2)}, u32[]{:S(2)}) collective-permute-start(f32[1,4,128,128]{3,2,1,0:T(8,128)} %fusion.37), channel_id=1, source_target_pairs={{32,0},{64,32},{96,64},{128,96},{160,128},{192,160},{224,192},{256... | collective-permute-start | bytes 786440 | tf_op jit(solution)/shard_map/ppermute | solution.py:17
  50.2 6.5 collective-permute-start.8
  54.2 7.6 collective-permute-start.9
  67.6 13.1 %collective-permute-start.10 = (f32[1,4,128,128]{3,2,1,0:T(8,128)}, f32[1,4,128,128]{3,2,1,0:T(8,128)}, u32[]{:S(2)}, u32[]{:S(2)}) collective-permute-start(f32[1,4,128,128]{3,2,1,0:T(8,128)} %fusion.34), channel_id=1, source_target_pairs={{0,32},{32,64},{64,96},{96,128},{128,160},{160,192},{192,224},{224... | collective-permute-start | bytes 786440 | tf_op jit(solution)/shard_map/ppermute | solution.py:16
  72.0 8.8 %collective-permute-start.11 = (f32[1,4,128,128]{3,2,1,0:T(8,128)}, f32[1,4,128,128]{3,2,1,0:T(8,128)}, u32[]{:S(2)}, u32[]{:S(2)}) collective-permute-start(f32[1,4,128,128]{3,2,1,0:T(8,128)} %fusion.34), channel_id=1, source_target_pairs={{32,0},{64,32},{96,64},{128,96},{160,128},{192,160},{224,192},{256... | collective-permute-start | bytes 786440 | tf_op jit(solution)/shard_map/ppermute | solution.py:17
  74.3 700.6 %all-reduce.23.cloned.1.call-start = ((), (), s32[]{:S(2)}) async-start(), calls=%async_computation | async-start | bytes 524288
  74.4 12.9 %copy-start.6 = (f32[1,4,128,128]{3,2,1,0:T(8,128)S(1)}, f32[1,4,128,128]{3,2,1,0:T(8,128)}, u32[]{:S(2)}) copy-start(f32[1,4,128,128]{3,2,1,0:T(8,128)} %copy-done.5) | copy-start | bytes 786436
  75.4 6.6 collective-permute-start.12
  79.5 7.8 collective-permute-start.13
  92.5 19.6 %copy-start.4 = (f32[1,4,128,128]{3,2,1,0:T(8,128)}, f32[1,4,128,128]{3,2,1,0:T(8,128)S(1)}, u32[]{:S(2)}) copy-start(f32[1,4,128,128]{3,2,1,0:T(8,128)S(1)} %fusion.31) | copy-start | bytes 786436
  92.5 12.0 %collective-permute-start.14 = (f32[1,4,128,128]{3,2,1,0:T(8,128)S(1)}, f32[1,4,128,128]{3,2,1,0:T(8,128)S(1)}, u32[]{:S(2)}, u32[]{:S(2)}) collective-permute-start(f32[1,4,128,128]{3,2,1,0:T(8,128)S(1)} %fusion.31), channel_id=1, source_target_pairs={{0,32},{32,64},{64,96},{96,128},{128,160},{160,192},{192,224},{224... | collective-permute-start | bytes 786440 | tf_op jit(solution)/shard_map/ppermute | solution.py:16
  96.7 7.9 %collective-permute-start.15 = (f32[1,4,128,128]{3,2,1,0:T(8,128)S(1)}, f32[1,4,128,128]{3,2,1,0:T(8,128)S(1)}, u32[]{:S(2)}, u32[]{:S(2)}) collective-permute-start(f32[1,4,128,128]{3,2,1,0:T(8,128)S(1)} %fusion.31), channel_id=1, source_target_pairs={{32,0},{64,32},{96,64},{128,96},{160,128},{192,160},{224,192},{256... | collective-permute-start | bytes 786440 | tf_op jit(solution)/shard_map/ppermute | solution.py:17
  98.7 7.8 collective-permute-start.16
  103.3 8.9 %collective-permute-start.17 = (f32[1,2,128,128]{3,2,1,0:T(8,128)S(1)}, f32[1,2,128,128]{3,2,1,0:T(8,128)S(1)}, u32[]{:S(2)}, u32[]{:S(2)}) collective-permute-start(f32[1,2,128,128]{3,2,1,0:T(8,128)S(1)} %get-tuple-element.13), channel_id=1, source_target_pairs={{32,0},{64,32},{96,64},{128,96},{160,128},{192,160},{224,192},{256... | collective-permute-start | bytes 393224 | tf_op jit(solution)/shard_map/ppermute | solution.py:17
  (14 other events, 63.4 us)
Sparse Core Ops, SparseCore 0:
  74.4 359.0 all-reduce.24
  437.4 337.4 all-reduce.22
where the time goes:
time: 784 us; the launch traced here: 783 us
  waiting for transfers between devices  678 us (86%)
  starting transfers between devices  49.7 us (6%)
  other arithmetic  26.7 us (3%)
  between operations  19.1 us (2%)
  local copies, waits for them, and re-layouts  9.72 us (1%)
    unnamed x3, waiting for transfers between devices  336 us
    psum x1, waiting for transfers between devices, from_root(): return lax.psum(block, axis)  319 us
    ppermute x9, starting transfers between devices, extended(): before = lax.ppermute(last, axis, up)  38 us
    ppermute x9, waiting for transfers between devices, extended(): after = lax.ppermute(leading, axis, down)  21.6 us
  transfers between devices with their start and end apart: 20, of which 8 were waited for; matrix products, arithmetic and copies ran while one was open for 2% of the time, Pallas kernels for 0%

commit v1 on v0

--- a/solution.py
+++ b/solution.py
@@ -4,6 +4,11 @@
 from jax.sharding import PartitionSpec as P
 
 SNAPS = 4
+
+
+def tiles_detail(patch, axis_key):
+    next_value = lax.all_gather(patch, axis_name=axis_key)
+    return jnp.sum(next_value, 0)
 
 
 def extended(shard, sides, width):
@@ -21,7 +26,7 @@
 
 def from_root(block, axis, owner):
     block = jnp.where(lax.axis_index(axis) == owner, block, jnp.zeros_like(block))
-    return lax.psum(block, axis)
+    return tiles_detail(block, axis)
 
 
 def piece_of(field, axis_no, begin, extent):

time: 784 us -> 924 us (1.18)
  waiting for transfers between devices: 678 us -> 788 us
  starting transfers between devices: 49.7 us -> 70.6 us
    all_gather x0 -> x4, waiting for transfers between devices: none -> 445 us  [tiles_detail(): next_value = lax.all_gather(patch, axis_name=axis_key)]
    psum x1 -> x0, waiting for transfers between devices: 319 us -> none  [from_root(): return lax.psum(block, axis)]
    ppermute x9, starting transfers between devices: 38 us -> 58.8 us  [extended(): before = lax.ppermute(last, axis, up)]
    ppermute x9, waiting for transfers between devices: 21.6 us -> 3.06 us  [extended(): after = lax.ppermute(leading, axis, down)]
    reduce_sum x0 -> x4, other arithmetic: none -> 18.1 us  [tiles_detail(): return jnp.sum(next_value, 0)]
    unnamed x3 -> x6, waiting for transfers between devices: 336 us -> 337 us
  transfers between devices with their start and end apart: 20 -> 23, of which waited for: 8 -> 12; matrix products, arithmetic and copies ran while one was open for 2% -> 3% of each run, Pallas kernels for 0% -> 0%
where the time goes in v1:
time: 924 us; the launch traced here: 923 us
  waiting for transfers between devices  788 us (85%)
  starting transfers between devices  70.6 us (8%)
  other arithmetic  35.8 us (4%)
  between operations  18.8 us (2%)
  local copies, waits for them, and re-layouts  9.36 us (1%)
    all_gather x4, waiting for transfers between devices, tiles_detail(): next_value = lax.all_gather(patch, axis_name=axis_key)  445 us
    unnamed x6, waiting for transfers between devices  337 us
    ppermute x9, starting transfers between devices, extended(): before = lax.ppermute(last, axis, up)  58.8 us
  transfers between devices with their start and end apart: 23, of which 12 were waited for; matrix products, arithmetic and copies ran while one was open for 3% of the time, Pallas kernels for 0%

profile of v1, /device:TPU:1, one launch (start us, length us, event | category | flops | bytes accessed | tf_op | source)
XLA Modules:
  0.0 923.1 jit_solution(7897160453166045373)
XLA Ops:
  11.2 2.0 broadcast_select_fusion.3
  15.3 4.0 collective-permute-start
  22.0 4.6 collective-permute-start.4
  30.9 4.0 collective-permute-start.2
  39.0 3.4 fusion.12
  44.8 7.0 collective-permute-start.6
  53.2 4.0 collective-permute-start.8
  59.4 1.7 fusion.15
  63.6 16.5 %collective-permute-start.10 = (f32[1,4,128,128]{3,2,1,0:T(8,128)S(1)}, f32[1,4,128,128]{3,2,1,0:T(8,128)S(1)}, u32[]{:S(2)}, u32[]{:S(2)}) collective-permute-start(f32[1,4,128,128]{3,2,1,0:T(8,128)S(1)} %fusion.38), channel_id=1, source_target_pairs={{0,32},{32,64},{64,96},{96,128},{128,160},{160,192},{192,224},{224... | collective-permute-start | bytes 786440 | tf_op jit(solution)/shard_map/ppermute | solution.py:21
  81.4 6.1 collective-permute-start.12
  89.7 1.8 fusion.18
  93.9 6.4 collective-permute-start.14
  102.3 6.2 collective-permute-start.16
  110.2 1.8 fusion.21
  112.1 23.8 %all-gather.11.cloned.1.call-done = f32[32,4,128,128]{3,2,1,0:T(8,128)} async-done(((f32[1,4,128,128]{3,2,1,0:T(8,128)}), f32[32,4,128,128]{3,2,1,0:T(8,128)}) %all-gather.11.cloned.1.call-update) | async-done | bytes 8388624 | tf_op jit(solution)/shard_map/all_gather | solution.py:10
  135.8 4.5 reduce_sum.41
  140.4 161.5 %all-gather.9.cloned.1.call-done = f32[32,4,128,128]{3,2,1,0:T(8,128)} async-done(((f32[1,4,128,128]{3,2,1,0:T(8,128)}), f32[32,4,128,128]{3,2,1,0:T(8,128)}) %all-gather.9.cloned.1.call-update) | async-done | bytes 8388624 | tf_op jit(solution)/shard_map/all_gather | solution.py:10
  301.8 4.5 reduce_sum.37
  306.4 129.5 %all-gather.7.cloned.1.call-done = f32[32,4,128,128]{3,2,1,0:T(8,128)} async-done(((f32[1,4,128,128]{3,2,1,0:T(8,128)}), f32[32,4,128,128]{3,2,1,0:T(8,128)}) %all-gather.7.cloned.1.call-update) | async-done | bytes 8388624 | tf_op jit(solution)/shard_map/all_gather | solution.py:10
  435.9 4.5 reduce_sum.36
  440.4 130.0 %all-gather.5.cloned.1.call-done = f32[32,4,128,128]{3,2,1,0:T(8,128)} async-done(((f32[1,4,128,128]{3,2,1,0:T(8,128)}), f32[32,4,128,128]{3,2,1,0:T(8,128)}) %all-gather.5.cloned.1.call-update) | async-done | bytes 8388624 | tf_op jit(solution)/shard_map/all_gather | solution.py:10
  570.3 4.5 reduce_sum.35
  574.9 3.3 fusion.27
  580.1 335.2 %all-reduce.21.cloned.1.call-done = f32[4,128,128]{2,1,0:T(8,128)} async-done(((f32[4,128,128]{2,1,0:T(8,128)}), f32[4,128,128]{2,1,0:T(8,128)}) %all-reduce.21.cloned.1.call-update) | async-done | bytes 262160
  (91 shorter events, 33.6 us)
Async XLA Ops:
  7.2 128.6 %all-gather.11.cloned.1.call-start = ((), (), s32[]{:S(2)}) async-start(), calls=%async_computation.3 | async-start | bytes 8650752 | tf_op jit(solution)/shard_map/all_gather | solution.py:10
  13.2 288.6 %all-gather.9.cloned.1.call-start = ((), (), s32[]{:S(2)}) async-start(), calls=%async_computation.2 | async-start | bytes 8650752 | tf_op jit(solution)/shard_map/all_gather | solution.py:10
  13.9 421.9 %all-gather.7.cloned.1.call-start = ((), (), s32[]{:S(2)}) async-start(), calls=%async_computation.1 | async-start | bytes 8650752 | tf_op jit(solution)/shard_map/all_gather | solution.py:10
  14.7 555.7 %all-gather.5.cloned.1.call-start = ((), (), s32[]{:S(2)}) async-start(), calls=%async_computation | async-start | bytes 8650752 | tf_op jit(solution)/shard_map/all_gather | solution.py:10
  15.2 900.0 %all-reduce.21.cloned.1.call-start = ((), (), s32[]{:S(2)}) async-start(), calls=%async_computation.4 | async-start | bytes 524288
  15.3 14.9 %collective-permute-start = (f32[1,4,128,128]{3,2,1,0:T(8,128)S(1)}, f32[1,4,128,128]{3,2,1,0:T(8,128)S(1)}, u32[]{:S(2)}, u32[]{:S(2)}) collective-permute-start(f32[1,4,128,128]{3,2,1,0:T(8,128)S(1)} %copy-done.7), channel_id=1, source_target_pairs={{0,32},{32,64},{64,96},{96,128},{128,160},{160,192},{192,224},{224... | collective-permute-start | bytes 786440 | tf_op jit(solution)/shard_map/ppermute | solution.py:21
  19.4 16.6 %collective-permute-start.1 = (f32[1,4,128,128]{3,2,1,0:T(8,128)S(1)}, f32[1,4,128,128]{3,2,1,0:T(8,128)}, u32[]{:S(2)}, u32[]{:S(2)}) collective-permute-start(f32[1,4,128,128]{3,2,1,0:T(8,128)S(1)} %copy-done.7), channel_id=1, source_target_pairs={{32,0},{64,32},{96,64},{128,96},{160,128},{192,160},{224,192},{256... | collective-permute-start | bytes 786440 | tf_op jit(solution)/shard_map/ppermute | solution.py:22
  20.7 16.3 %collective-permute-start.5 = (f32[2,4,128,128]{3,2,1,0:T(8,128)S(1)}, f32[2,4,128,128]{3,2,1,0:T(8,128)S(1)}, u32[]{:S(2)}, u32[]{:S(2)}) collective-permute-start(f32[2,4,128,128]{3,2,1,0:T(8,128)S(1)} %pad_maximum_fusion.8), channel_id=1, source_target_pairs={{32,0},{64,32},{96,64},{128,96},{160,128},{192,160},{224,192},{256... | collective-permute-start | bytes 1572872 | tf_op jit(solution)/shard_map/ppermute | solution.py:22
  22.0 15.0 %collective-permute-start.4 = (f32[2,4,128,128]{3,2,1,0:T(8,128)S(1)}, f32[2,4,128,128]{3,2,1,0:T(8,128)S(1)}, u32[]{:S(2)}, u32[]{:S(2)}) collective-permute-start(f32[2,4,128,128]{3,2,1,0:T(8,128)S(1)} %pad_maximum_fusion.8), channel_id=1, source_target_pairs={{0,32},{32,64},{64,96},{96,128},{128,160},{160,192},{192,224},{224... | collective-permute-start | bytes 1572872 | tf_op jit(solution)/shard_map/ppermute | solution.py:21
  27.4 11.5 %collective-permute-start.3 = (f32[1,2,128,128]{3,2,1,0:T(8,128)}, f32[1,2,128,128]{3,2,1,0:T(8,128)}, u32[]{:S(2)}, u32[]{:S(2)}) collective-permute-start(f32[1,2,128,128]{3,2,1,0:T(8,128)} %get-tuple-element.22), channel_id=1, source_target_pairs={{32,0},{64,32},{96,64},{128,96},{160,128},{192,160},{224,192},{256... | collective-permute-start | bytes 393224 | tf_op jit(solution)/shard_map/ppermute | solution.py:22
  30.9 8.0 collective-permute-start.2
  43.5 13.7 %collective-permute-start.7 = (f32[1,4,128,128]{3,2,1,0:T(8,128)S(1)}, f32[1,4,128,128]{3,2,1,0:T(8,128)S(1)}, u32[]{:S(2)}, u32[]{:S(2)}) collective-permute-start(f32[1,4,128,128]{3,2,1,0:T(8,128)S(1)} %fusion.41), channel_id=1, source_target_pairs={{32,0},{64,32},{96,64},{128,96},{160,128},{192,160},{224,192},{256... | collective-permute-start | bytes 786440 | tf_op jit(solution)/shard_map/ppermute | solution.py:22
  44.8 12.4 %collective-permute-start.6 = (f32[1,4,128,128]{3,2,1,0:T(8,128)S(1)}, f32[1,4,128,128]{3,2,1,0:T(8,128)S(1)}, u32[]{:S(2)}, u32[]{:S(2)}) collective-permute-start(f32[1,4,128,128]{3,2,1,0:T(8,128)S(1)} %fusion.41), channel_id=1, source_target_pairs={{0,32},{32,64},{64,96},{96,128},{128,160},{160,192},{192,224},{224... | collective-permute-start | bytes 786440 | tf_op jit(solution)/shard_map/ppermute | solution.py:21
  51.9 6.4 collective-permute-start.9
  53.2 6.2 collective-permute-start.8
  62.3 25.2 %collective-permute-start.11 = (f32[1,4,128,128]{3,2,1,0:T(8,128)S(1)}, f32[1,4,128,128]{3,2,1,0:T(8,128)S(1)}, u32[]{:S(2)}, u32[]{:S(2)}) collective-permute-start(f32[1,4,128,128]{3,2,1,0:T(8,128)S(1)} %fusion.38), channel_id=1, source_target_pairs={{32,0},{64,32},{96,64},{128,96},{160,128},{192,160},{224,192},{256... | collective-permute-start | bytes 786440 | tf_op jit(solution)/shard_map/ppermute | solution.py:22
  63.6 23.9 %collective-permute-start.10 = (f32[1,4,128,128]{3,2,1,0:T(8,128)S(1)}, f32[1,4,128,128]{3,2,1,0:T(8,128)S(1)}, u32[]{:S(2)}, u32[]{:S(2)}) collective-permute-start(f32[1,4,128,128]{3,2,1,0:T(8,128)S(1)} %fusion.38), channel_id=1, source_target_pairs={{0,32},{32,64},{64,96},{96,128},{128,160},{160,192},{192,224},{224... | collective-permute-start | bytes 786440 | tf_op jit(solution)/shard_map/ppermute | solution.py:21
  80.1 8.2 collective-permute-start.13
  81.4 8.3 collective-permute-start.12
  92.6 15.8 %collective-permute-start.15 = (f32[1,4,128,128]{3,2,1,0:T(8,128)S(1)}, f32[1,4,128,128]{3,2,1,0:T(8,128)S(1)}, u32[]{:S(2)}, u32[]{:S(2)}) collective-permute-start(f32[1,4,128,128]{3,2,1,0:T(8,128)S(1)} %fusion.35), channel_id=1, source_target_pairs={{32,0},{64,32},{96,64},{128,96},{160,128},{192,160},{224,192},{256... | collective-permute-start | bytes 786440 | tf_op jit(solution)/shard_map/ppermute | solution.py:22
  93.9 14.6 %collective-permute-start.14 = (f32[1,4,128,128]{3,2,1,0:T(8,128)S(1)}, f32[1,4,128,128]{3,2,1,0:T(8,128)S(1)}, u32[]{:S(2)}, u32[]{:S(2)}) collective-permute-start(f32[1,4,128,128]{3,2,1,0:T(8,128)S(1)} %fusion.35), channel_id=1, source_target_pairs={{0,32},{32,64},{64,96},{96,128},{128,160},{160,192},{192,224},{224... | collective-permute-start | bytes 786440 | tf_op jit(solution)/shard_map/ppermute | solution.py:21
  101.0 8.1 collective-permute-start.17
  102.3 7.9 collective-permute-start.16
  440.4 134.5 %slice-start = ((f32[1,8,128,128]{3,2,1,0:T(8,128)}), f32[1,4,128,128]{3,2,1,0:T(8,128)S(1)}, s32[]{:S(2)}) async-start(f32[1,8,128,128]{3,2,1,0:T(8,128)} %copy-done.1), calls=%async_computation.5 | async-start | bytes 524288 | tf_op jit(solution)/shard_map/slice | solution.py:33
  (10 other events, 231.5 us)
Sparse Core Ops, SparseCore 0:
  13.3 122.4 all-gather.10
  139.0 162.8 all-gather.8
  305.0 130.8 all-gather.6
  439.4 130.8 all-gather.4
  578.3 336.9 all-reduce.20
